TPU v7x, 256 devices: a whole 4x4x8 slice. The times are simulated.
256 devices in a mesh: species: 16 (over z_hi, y, core), series: 16 (over z_lo, x).
Axes of the slice: x: 4, y: 4, z: 8 (z_hi: 2, z_lo: 4; z = z_hi * 4 + z_lo), core: 2. Of those that a mesh axis runs over, the one named last changes fastest.
Arguments:
- observed: bfloat16 [4096, 9216], P(('species', 'series')), may hold values from -6 to 6
- defocus: float32 [4096], P(('species', 'series')), may hold values from 1 to 4
- shift_center: int32 [2, 4096], P(None, ('species', 'series')), may hold values from -4 to 4
- pose_index: int32 [4096, 64], P(('species', 'series')), may hold values from 0 to 15
- pose_logprior: float32 [4096, 64], P(('species', 'series')), may hold values from -4 to 400
- reference_tiles: bfloat16 [512, 9216], P('species'), may hold values from -6 to 6
- series_id: int32 [4096], P(('species', 'series')), may hold values from 0 to 15
- tilt_id: int32 [4096], P(('species', 'series')), may hold values from 0 to 39
Outputs:
- item_loglik: float32 [4096], P(('species', 'series'))
- tilt_grads: float32 [3, 16, 40], P(None, 'series')
All inputs are finite; a program needn't handle non-finite values.
Results may differ from a plain program's by a relative error of at most 0.012.
Values may be sent and summed in bfloat16 or wider, within the bound.
A program may use at most 128 MiB of HBM per device.

v0:
```python
import functools
import math

import jax
import jax.numpy as jnp
import ml_dtypes
import numpy as np
from jax import lax
from jax.experimental import pallas as pl
from jax.experimental.pallas import tpu as pltpu
from jax.sharding import PartitionSpec as P

MESH = pl.DeviceIdType.MESH
F32 = jnp.float32
BF16 = jnp.bfloat16

BOX = 96
FREQ = 4608
SHIFT_Y = 8
SHIFT_X = 16
POSES_SP = 16
TILTS = 40
SCORE_SCALE = 0.03125
CTF_RATE = 4.0
AMP_PHASE = 0.1
ENV_RATE = 0.5
TWO_PI = 6.283185307179586

GROUPS = 6
WIDTH = FREQ // GROUPS
BLOCKS = GROUPS // 2
DEPTH = 2 * WIDTH
SUB = 256
LANES = 128
ITEMS = 16
NY = 4
NX = 4
NZ = 8
UNIT = WIDTH // 2
PAIRS = 8
ROWS = NY * PAIRS * ITEMS


def shift_halves():
    window = [(i - SHIFT_Y // 2, j - SHIFT_X // 2) for i in range(SHIFT_Y) for j in range(SHIFT_X)]
    inside = set(window)
    both = [s for s in window if s > (0, 0) and (-s[0], -s[1]) in inside]
    alone = [(0, 0)] + [s for s in window if (-s[0], -s[1]) not in inside]
    return both, alone


BOTH, ALONE = shift_halves()
N_BOTH, N_HALF = len(BOTH), len(BOTH) + len(ALONE)


def sine_fit():
    turn = np.cos(np.pi * (np.arange(400) + 0.5) / 400) * 0.5
    square = turn * turn
    odd = np.stack([turn * square**k for k in range(6)], 1)
    even = np.stack([square**k for k in range(7)], 1)
    sine = np.linalg.lstsq(odd, np.sin(2 * np.pi * turn), rcond=None)[0]
    cosine = np.linalg.lstsq(even, np.cos(2 * np.pi * turn), rcond=None)[0]
    return [float(np.float32(c)) for c in sine], [float(np.float32(c)) for c in cosine]


SINE, COSINE = sine_fit()


def sin_cos(turns):
    turn = turns - jnp.floor(turns + 0.5)
    square = turn * turn
    sine = SINE[-1]
    for c in SINE[-2::-1]:
        sine = sine * square + c
    cosine = COSINE[-1]
    for c in COSINE[-2::-1]:
        cosine = cosine * square + c
    return sine * turn, cosine


def frequencies():
    flat = np.arange(FREQ)
    row, col = flat // (BOX // 2), flat % (BOX // 2)
    return np.where(row < BOX // 2, row, row - BOX).astype(np.float64), col.astype(np.float64)


def frequency_rows():
    freq_y, freq_x = frequencies()
    k2 = (freq_y**2 + freq_x**2) / (BOX / 2.0) ** 2
    env = np.exp(-ENV_RATE * k2)
    rows = np.zeros((8, FREQ), np.float64)
    rows[0] = freq_y
    rows[1] = freq_x
    rows[2] = CTF_RATE * k2 / TWO_PI
    rows[3] = -env
    rows[4] = -CTF_RATE * k2 * env
    return rows.astype(np.float32)


def phase_tables():
    freq_y, freq_x = frequencies()
    half = np.array(BOTH + ALONE, np.float64)
    angle = TWO_PI / BOX * (freq_y[:, None] * half[None, :, 0] + freq_x[:, None] * half[None, :, 1])
    cosine, sine = np.cos(angle), np.sin(angle)
    rate_x, rate_y = (TWO_PI / BOX * freq_x)[:, None], (TWO_PI / BOX * freq_y)[:, None]
    table = np.zeros((2, FREQ, 2 * LANES), np.float64)
    slopes = np.zeros((2, FREQ, LANES), np.float64)
    for part, (value, slope) in enumerate(((cosine, -sine), (sine, cosine))):
        table[part, :, :N_HALF] = value
        table[part, :, N_HALF : N_HALF + N_BOTH] = rate_x * slope[:, :N_BOTH]
        table[part, :, LANES : LANES + N_HALF] = rate_y * slope
        table[part, :, LANES + N_HALF : LANES + 2 * N_HALF - N_BOTH] = rate_x * slope[:, N_BOTH:]
        slopes[part, :, :N_HALF] = value
        slopes[part, :, N_HALF:] = (1 - 2 * part) * value[:, :N_BOTH]
    table = table.reshape(2, BLOCKS, DEPTH, 2 * LANES).transpose(1, 0, 2, 3)
    slopes = slopes.reshape(2, BLOCKS, DEPTH, LANES).transpose(1, 0, 2, 3).reshape(BLOCKS, 2 * DEPTH, LANES)
    return [t.astype(np.float32).astype(ml_dtypes.bfloat16) for t in (table, slopes)]


def kernel(
    observed,
    reference_tiles,
    table_in,
    slopes_in,
    freq_rows,
    pose_index,
    pose_logprior,
    defocus,
    shift_center,
    series_id,
    tilt_id,
    result,
    raw,
    tiles,
    items,
    table,
    slopes,
    ext,
    priors,
    pose_hot,
    ctf,
    lhs,
    lhs_slope,
    acc,
    acc_slope,
    part_out,
    part_in,
    own_loglik,
    xc_out,
    xc_in,
    z_out,
    z_in,
    local_sem,
    table_sem,
    item_send,
    item_recv,
    near_send,
    near_recv,
    far_send,
    far_recv,
    sib_send,
    sib_recv,
    ext_send,
    ext_recv,
    part_send,
    part_recv,
    xc_send,
    xc_recv,
    z_send,
    z_recv,
):
    sp = lax.axis_index("species")
    se = lax.axis_index("series")
    z_hi, y, core = sp // 8, (sp // 2) % NY, sp % 2
    z_lo, x = se // NX, se % NX
    z, xc = z_hi * 4 + z_lo, x * 2 + core

    def at_y(other):
        return (z_hi * 8 + other * 2 + core, se)

    def at_z(other):
        return (other // 4 * 8 + y * 2 + core, other % 4 * NX + x)

    def at_xc(other):
        return (z_hi * 8 + y * 2 + other % 2, z_lo * NX + other // 2)

    sibling = (z_hi * 8 + y * 2 + 1 - core, se)
    mirror = at_z(NZ - 1 - z)
    own_tiles = z_hi * 2 + core
    own_far = (1 - z_hi) * 2 + core
    sibling_tiles = z_hi * 2 + 1 - core
    sibling_far = (1 - z_hi) * 2 + 1 - core

    barrier = pltpu.get_barrier_semaphore()
    partners = [at_y((y + k) % NY) for k in range(1, NY)]
    partners += [at_xc((xc + k) % (2 * NX)) for k in range(1, 2 * NX)]
    partners += [at_z((z + k) % NZ) for k in range(1, NZ)]
    for partner in partners:
        pl.semaphore_signal(barrier, inc=1, device_id=partner, device_id_type=MESH)

    raw_copy = pltpu.make_async_copy(observed, raw, local_sem.at[2 * GROUPS])
    raw_copy.start()

    def tile_copy(g, part):
        return pltpu.make_async_copy(
            reference_tiles.at[:, pl.ds(pl.multiple_of(part * FREQ + g * WIDTH, WIDTH), WIDTH)],
            tiles.at[g, own_tiles, part],
            local_sem.at[2 * g + part],
        )

    def table_copy(k):
        return pltpu.make_async_copy(table_in.at[k], table.at[k], table_sem.at[k])

    def slopes_copy(k):
        return pltpu.make_async_copy(slopes_in.at[k], slopes.at[k], table_sem.at[BLOCKS + k])

    @pl.loop(0, GROUPS)
    def _(g):
        tile_copy(g, 0).start()
        tile_copy(g, 1).start()

    def remote(src, dst, send, recv, device):
        return pltpu.make_async_remote_copy(
            src_ref=src, dst_ref=dst, send_sem=send, recv_sem=recv, device_id=device, device_id_type=MESH
        )

    def send_item(k, g):
        ref = items.at[g, y]
        return remote(ref, ref, item_send.at[k, g], item_recv.at[k, g], at_y((y + k) % NY))

    def take_item(k, g):
        other = (y + NY - k) % NY
        ref = items.at[g, other]
        return remote(ref, ref, item_send.at[k, g], item_recv.at[k, g], at_y(other))

    def send_near(g):
        ref = tiles.at[g, own_tiles]
        return remote(ref, ref, near_send.at[g], near_recv.at[g], sibling)

    def take_near(g):
        ref = tiles.at[g, sibling_tiles]
        return remote(ref, ref, near_send.at[g], near_recv.at[g], sibling)

    def unit(slot, u):
        return tiles.at[u // 2, slot, :, :, pl.ds(pl.multiple_of(u % 2 * UNIT, UNIT), UNIT)]

    def send_mirror(k):
        ref, u = unit(own_tiles, NX * k + x), NX * k + x
        return remote(ref, ref, far_send.at[0, k], far_recv.at[u], mirror)

    def send_x(j, k):
        ref, u = unit(own_far, NX * k + x), NX * k + x
        return remote(ref, ref, far_send.at[j, k], far_recv.at[u], (sp, z_lo * NX + (x + j) % NX))

    def take_far(j, k):
        u = NX * k + (x + j) % NX
        ref = unit(own_far, u)
        return remote(ref, ref, far_send.at[j, k], far_recv.at[u], mirror)

    def send_sibling(u):
        ref = unit(own_far, u)
        return remote(ref, ref, sib_send.at[u], sib_recv.at[u], sibling)

    def take_sibling(u):
        ref = unit(sibling_far, u)
        return remote(ref, ref, sib_send.at[u], sib_recv.at[u], sibling)

    def send_ext(k):
        ref = ext.at[y]
        return remote(ref, ref, ext_send.at[k], ext_recv.at[k], at_y((y + k) % NY))

    def take_ext(k):
        other = (y + NY - k) % NY
        ref = ext.at[other]
        return remote(ref, ref, ext_send.at[k], ext_recv.at[k], at_y(other))

    row16 = lax.broadcasted_iota(jnp.int32, (ITEMS, LANES), 0)
    lane16 = lax.broadcasted_iota(jnp.int32, (ITEMS, LANES), 1)

    def column(read):
        out = jnp.zeros((ITEMS, LANES), F32)
        for n in range(ITEMS):
            out = jnp.where(row16 == n, read(n).astype(F32), out)
        return out

    ext[y, :ITEMS, :] = jnp.concatenate([pose_index[...].astype(F32), pose_logprior[...]], 1)
    facts = jnp.where(lane16 == 0, column(lambda n: defocus[n]), column(lambda n: tilt_id[n]))
    ext[y, ITEMS:, :] = jnp.where(lane16 == 2, column(lambda n: series_id[n]), facts)

    center_y = column(lambda n: shift_center[0, n])
    center_x = column(lambda n: shift_center[1, n])
    center_y = jnp.concatenate([center_y, center_y], 1)
    center_x = jnp.concatenate([center_x, center_x], 1)
    pl.semaphore_wait(barrier, len(partners))

    for k in (2, 1, 3):
        send_ext(k).start()
    raw_copy.wait()

    @pl.loop(0, GROUPS)
    def _(g):
        for sub in range(WIDTH // SUB):
            at = g * WIDTH + sub * SUB
            re_cols = pl.ds(pl.multiple_of(at, SUB), SUB)
            im_cols = pl.ds(pl.multiple_of(FREQ + at, SUB), SUB)
            turns = freq_rows[0:1, re_cols] * center_y + freq_rows[1:2, re_cols] * center_x
            sine, cosine = sin_cos(turns * (1.0 / BOX))
            re, im = raw[:, re_cols].astype(F32), raw[:, im_cols].astype(F32)
            cols = slice(sub * SUB, (sub + 1) * SUB)
            items[g, y, 0, :, cols] = (re * cosine + im * sine).astype(BF16)
            items[g, y, 1, :, cols] = (im * cosine - re * sine).astype(BF16)
        for k in (2, 1, 3):
            send_item(k, g).start()
        tile_copy(g, 0).wait()
        tile_copy(g, 1).wait()

        for half in range(2):

            @pl.when((2 * g + half) % NX == x)
            def _(half=half):
                send_mirror((2 * g + half) // NX).start()

        send_near(g).start()

    for k in range(BLOCKS):
        table_copy(k).start()
        slopes_copy(k).start()
    acc[...] = jnp.zeros_like(acc)
    acc_slope[...] = jnp.zeros_like(acc_slope)

    lane_f = lane16.astype(F32)
    to_front = (LANES - 8 * y) % LANES

    @pl.loop(0, NY)
    def _(k):
        @pl.when(k > 0)
        def _():
            take_ext(k).wait_recv()

        b = (y + NY - k) % NY
        moved = pltpu.roll(ext[b, :ITEMS, :], to_front, 1)
        priors[b] = moved
        for h in range(2):
            for j in range(PAIRS):
                pose = moved[:, 32 * h + j : 32 * h + j + 1] + float((j // 2) * POSES_SP)
                hot = jnp.where(lane_f == pose, 1.0, 0.0)[:, : 4 * POSES_SP]
                pose_hot[h, b, j * ITEMS : (j + 1) * ITEMS, :] = hot.astype(BF16)
        focus = ext[b, ITEMS:, 0:1] + jnp.zeros((ITEMS, WIDTH), F32)

        @pl.loop(0, GROUPS)
        def _(g):
            cols = pl.ds(pl.multiple_of(g * WIDTH, WIDTH), WIDTH)
            turns = focus * freq_rows[2:3, cols] - AMP_PHASE / TWO_PI
            sine, cosine = sin_cos(turns)
            ctf[0, b, :, cols] = (sine * freq_rows[3:4, cols]).astype(BF16)
            ctf[1, b, :, cols] = (cosine * freq_rows[4:5, cols]).astype(BF16)

    def pass_own(k):
        take_far(0, k).wait_recv()
        for j in (2, 1, 3):
            send_x(j, k).start()
        send_sibling(NX * k + x).start()

    def pass_other(k):
        for j in range(1, NX):
            take_far(j, k).wait_recv()
            send_sibling(NX * k + (x + j) % NX).start()

    def fill(g, h, part):
        for sub in range(WIDTH // SUB):
            cols = slice(sub * SUB, (sub + 1) * SUB)
            tile_re = tiles[g, pl.ds(2 * h, 2), 0, :, cols].reshape(4 * POSES_SP, SUB)
            tile_im = tiles[g, pl.ds(2 * h, 2), 1, :, cols].reshape(4 * POSES_SP, SUB)
            freqs = pl.ds(pl.multiple_of(g * WIDTH + sub * SUB, SUB), SUB)
            at = part * WIDTH + sub * SUB
            for b in range(NY):
                hot = pose_hot[h, b]
                re = jnp.dot(hot, tile_re, preferred_element_type=F32).reshape(PAIRS, ITEMS, SUB).astype(BF16)
                im = jnp.dot(hot, tile_im, preferred_element_type=F32).reshape(PAIRS, ITEMS, SUB).astype(BF16)
                value, slope = ctf[0, b, :, freqs], ctf[1, b, :, freqs]
                o_re, o_im = items[g, b, 0, :, cols], items[g, b, 1, :, cols]
                prod_re = re * o_re + im * o_im
                prod_im = re * o_im - im * o_re
                rows = slice(b * PAIRS * ITEMS, (b + 1) * PAIRS * ITEMS)
                lhs[0, rows, at : at + SUB] = (prod_re * value).reshape(PAIRS * ITEMS, SUB)
                lhs[1, rows, at : at + SUB] = (prod_im * value).reshape(PAIRS * ITEMS, SUB)
                lhs_slope[rows, at : at + SUB] = (prod_re * slope).reshape(PAIRS * ITEMS, SUB)
                lhs_slope[rows, DEPTH + at : DEPTH + at + SUB] = (prod_im * slope).reshape(PAIRS * ITEMS, SUB)

    passing = ((0, 0, 0, True), (0, 1, 1, True), (1, 0, 2, True), (1, 1, 0, False), (2, 0, 1, False), (2, 1, 2, False))

    @pl.loop(0, 2 * BLOCKS)
    def _(i):
        far = jnp.where(i < 2, 0, jnp.where(i == 3, 0, 1))
        block = jnp.where(i < 2, i, jnp.where(i == 2, 0, jnp.where(i == 3, 2, i - 3)))
        h = (z_hi + far) % 2
        for part in range(2):
            g = 2 * block + part

            @pl.when(far == 0)
            def _(g=g):
                for k in range(1, NY):
                    take_item(k, g).wait_recv()
                take_near(g).wait_recv()

            @pl.when(far == 1)
            def _(g=g):
                take_sibling(2 * g).wait_recv()
                take_sibling(2 * g + 1).wait_recv()

            fill(g, h, part)
            for at, at_part, k, own in passing:
                if at_part == part:

                    @pl.when(i == at)
                    def _(k=k, own=own):
                        if own:
                            pass_own(k)
                        else:
                            pass_other(k)

        @pl.when(far == 0)
        def _():
            table_copy(block).wait()
            slopes_copy(block).wait()

        for q in range(2):
            acc[h, q] += jnp.dot(lhs[q], table[block, q], preferred_element_type=F32)
        acc_slope[h] += jnp.dot(lhs_slope[...], slopes[block], preferred_element_type=F32)

    plus_ok, minus_ok = lane16 < N_HALF, lane16 < N_BOTH
    lowest = -1e30
    part_out[...] = jnp.zeros_like(part_out)

    @pl.loop(0, NY)
    def _(b):
        message = priors[b]
        places = []
        for h in range(2):
            for j in range(PAIRS):
                places.append((h, j, pl.ds(pl.multiple_of((b * PAIRS + j) * ITEMS, ITEMS), ITEMS)))
        scores = []
        for h, j, rows in places:
            prior = message[:, 64 + 32 * h + j : 64 + 32 * h + j + 1]
            re, im = acc[h, 0, rows, :LANES], acc[h, 1, rows, :LANES]
            scores.append(
                (
                    jnp.where(plus_ok, SCORE_SCALE * (re + im) + prior, lowest),
                    jnp.where(minus_ok, SCORE_SCALE * (re - im) + prior, lowest),
                )
            )
        top = functools.reduce(jnp.maximum, [jnp.maximum(p, m) for p, m in scores])
        top = jnp.max(top, axis=1, keepdims=True)
        zero = jnp.zeros((ITEMS, LANES), F32)
        total, d_focus, d_x, d_x_alone, d_y = zero, zero, zero, zero, zero
        for (h, j, rows), (p, m) in zip(places, scores):
            p, m = jnp.exp(p - top), jnp.exp(m - top)
            total += p + m
            m_moved = pltpu.roll(m, N_HALF, 1)
            d_focus += (p + m_moved) * acc_slope[h, rows, :]
            re, im = acc[h, 0, rows, :LANES], acc[h, 1, rows, :LANES]
            d_x += pltpu.roll(p, N_HALF, 1) * (re + im) - m_moved * (re - im)
            re, im = acc[h, 0, rows, LANES:], acc[h, 1, rows, LANES:]
            d_y += p * (re + im) - m * (re - im)
            d_x_alone += pltpu.roll(p, N_HALF - N_BOTH, 1) * (re + im)
        d_x = jnp.where(lane16 >= N_HALF, d_x, 0.0)
        d_x += jnp.where((lane16 >= N_HALF) & (lane16 < 2 * N_HALF - N_BOTH), d_x_alone, 0.0)
        out = jnp.where(lane16 == 8 * b, top, part_out[...])
        for at, term in enumerate((total, d_focus, d_x, d_y)):
            out = jnp.where(lane16 == 8 * b + at + 1, jnp.sum(term, axis=1, keepdims=True), out)
        part_out[...] = out

    def send_part(k):
        other = (y + k) % NY
        return remote(part_out, part_in.at[y], part_send.at[k], part_recv.at[k], at_y(other))

    def take_part(k):
        other = (y + NY - k) % NY
        return remote(part_out, part_in.at[other], part_send.at[k], part_recv.at[k], at_y(other))

    for k in range(1, NY):
        send_part(k).start()
    part_in[y] = part_out[...]

    tilt, series = [], []
    for b in range(NY):
        tilt.append(ext[b, ITEMS:, 1:2] + jnp.zeros((ITEMS, LANES), F32))
        series.append(ext[b, ITEMS:, 2:3] + jnp.zeros((ITEMS, LANES), F32))
    for k in range(1, NY):
        take_part(k).wait_recv()

    placed = []
    for b in range(NY):
        parts = [part_in[src] for src in range(NY)]
        at_b = 8 * b
        tops = [part[:, at_b : at_b + 1] for part in parts]
        top = functools.reduce(jnp.maximum, tops)
        sums = sum(part * jnp.exp(t - top) for part, t in zip(parts, tops))
        total = sums[:, at_b + 1 : at_b + 2]
        grads = sums * SCORE_SCALE / total
        spread = jnp.zeros((ITEMS, LANES), F32)
        for at in range(3):
            spread = jnp.where(lane_f == tilt[b] + float(at * TILTS), grads[:, at_b + 2 + at : at_b + 3 + at], spread)
        placed.append(spread)
        own_loglik[b] = top + jnp.log(total) + jnp.zeros((ITEMS, LANES), F32)
    row8 = lax.broadcasted_iota(jnp.int32, (8, LANES), 0)
    for to in range(NX):
        rows = jnp.zeros((8, LANES), F32)
        for lo in range(4):
            hits = [jnp.where(s == float(lo * NX + to), p, 0.0) for s, p in zip(series, placed)]
            rows = jnp.where(row8 == lo, jnp.sum(sum(hits), axis=0, keepdims=True), rows)
        xc_out[to] = rows

    def send_xc(k):
        other = (xc + k) % (2 * NX)
        return remote(xc_out.at[other // 2], xc_in.at[xc], xc_send.at[k], xc_recv.at[k], at_xc(other))

    def take_xc(k):
        other = (xc + 2 * NX - k) % (2 * NX)
        return remote(xc_out.at[x], xc_in.at[other], xc_send.at[k], xc_recv.at[k], at_xc(other))

    for k in range(1, 2 * NX):
        send_xc(k).start()
    xc_in[xc] = xc_out[x]
    loglik = own_loglik[y]
    result[0:1, :] = jnp.sum(jnp.where(row16 == lane16, loglik, 0.0), axis=0, keepdims=True)
    for k in range(1, 2 * NX):
        take_xc(k).wait_recv()
    rows = sum(xc_in[k] for k in range(2 * NX))
    for lo in range(4):
        z_out[lo] = rows[lo : lo + 1]

    def send_z(k):
        other = (z + k) % NZ
        return remote(z_out.at[other % 4], z_in.at[z], z_send.at[k], z_recv.at[k], at_z(other))

    def take_z(k):
        other = (z + NZ - k) % NZ
        return remote(z_out.at[z_lo], z_in.at[other], z_send.at[k], z_recv.at[k], at_z(other))

    for k in range(1, NZ):
        send_z(k).start()
    z_in[z] = z_out[z_lo]
    for k in range(1, NZ):
        take_z(k).wait_recv()
    result[1:2, :] = sum(z_in[k] for k in range(NZ))

    for k in range(1, NY):
        send_ext(k).wait_send()

    @pl.loop(0, GROUPS)
    def _(g):
        for k in range(1, NY):
            send_item(k, g).wait_send()
        send_near(g).wait_send()
        send_sibling(2 * g).wait_send()
        send_sibling(2 * g + 1).wait_send()

    for k in range(GROUPS // 2):
        send_mirror(k).wait_send()
        for j in range(1, NX):
            send_x(j, k).wait_send()
    for k in range(1, NY):
        send_part(k).wait_send()

    for k in range(1, 2 * NX):
        send_xc(k).wait_send()
    for k in range(1, NZ):
        send_z(k).wait_send()


def finish(result, loglik_out, tilt_out):
    loglik_out[...] = result[0, :ITEMS]
    for at in range(3):
        tilt_out[at] = result[1:2, at * TILTS : (at + 1) * TILTS]


def solution(mesh):
    placed = (
        P(("species", "series"), None),
        P(("species", "series")),
        P(None, ("species", "series")),
        P(("species", "series"), None),
        P(("species", "series"), None),
        P("species", None),
        P(("species", "series")),
        P(("species", "series")),
    )
    table, slopes = phase_tables()
    rows = frequency_rows()
    any_space = pl.BlockSpec(memory_space=pl.ANY)
    vmem = pl.BlockSpec(memory_space=pltpu.VMEM)
    smem = pl.BlockSpec(memory_space=pltpu.SMEM)
    dma = pltpu.SemaphoreType.DMA

    def body(observed, defocus, shift_center, pose_index, pose_logprior, reference_tiles, series_id, tilt_id):
        result = pl.pallas_call(
            kernel,
            out_shape=jax.ShapeDtypeStruct((8, LANES), F32),
            in_specs=[any_space, any_space, any_space, any_space, vmem, vmem, vmem, smem, smem, smem, smem],
            out_specs=vmem,
            scratch_shapes=[
                pltpu.VMEM((ITEMS, 2 * FREQ), BF16),
                pltpu.VMEM((GROUPS, 4, 2, 2 * POSES_SP, WIDTH), BF16),
                pltpu.VMEM((GROUPS, NY, 2, ITEMS, WIDTH), BF16),
                pltpu.VMEM((BLOCKS, 2, DEPTH, 2 * LANES), BF16),
                pltpu.VMEM((BLOCKS, 2 * DEPTH, LANES), BF16),
                pltpu.VMEM((NY, 2 * ITEMS, LANES), F32),
                pltpu.VMEM((NY, ITEMS, LANES), F32),
                pltpu.VMEM((2, NY, PAIRS * ITEMS, 4 * POSES_SP), BF16),
                pltpu.VMEM((2, NY, ITEMS, FREQ), BF16),
                pltpu.VMEM((2, ROWS, DEPTH), BF16),
                pltpu.VMEM((ROWS, 2 * DEPTH), BF16),
                pltpu.VMEM((2, 2, ROWS, 2 * LANES), F32),
                pltpu.VMEM((2, ROWS, LANES), F32),
                pltpu.VMEM((ITEMS, LANES), F32),
                pltpu.VMEM((NY, ITEMS, LANES), F32),
                pltpu.VMEM((NY, ITEMS, LANES), F32),
                pltpu.VMEM((NX, 8, LANES), F32),
                pltpu.VMEM((2 * NX, 8, LANES), F32),
                pltpu.VMEM((4, 1, LANES), F32),
                pltpu.VMEM((NZ, 1, LANES), F32),
                dma((2 * GROUPS + 1,)),
                dma((2 * BLOCKS,)),
                dma((NY, GROUPS)),
                dma((NY, GROUPS)),
                dma((GROUPS,)),
                dma((GROUPS,)),
                dma((NX, GROUPS // 2)),
                dma((2 * GROUPS,)),
                dma((2 * GROUPS,)),
                dma((2 * GROUPS,)),
                dma((NY,)),
                dma((NY,)),
                dma((NY,)),
                dma((NY,)),
                dma((2 * NX,)),
                dma((2 * NX,)),
                dma((NZ,)),
                dma((NZ,)),
            ],
            compiler_params=pltpu.CompilerParams(
                collective_id=0, has_side_effects=True, vmem_limit_bytes=60 * 2**20
            ),
        )(
            observed,
            reference_tiles,
            jnp.asarray(table),
            jnp.asarray(slopes),
            jnp.asarray(rows),
            pose_index,
            pose_logprior,
            defocus,
            shift_center,
            series_id,
            tilt_id,
        )
        return pl.pallas_call(
            finish,
            out_shape=(jax.ShapeDtypeStruct((ITEMS,), F32), jax.ShapeDtypeStruct((3, 1, TILTS), F32)),
            in_specs=[vmem],
            out_specs=(vmem, vmem),
        )(result)

    return jax.shard_map(
        body,
        mesh=mesh,
        in_specs=placed,
        out_specs=(P(("species", "series")), P(None, "series", None)),
        check_vma=False,
    )
```

profile of v0, /device:TPU:1, one launch (start us, length us, event | category | flops | bytes accessed | tf_op | source)
XLA Modules:
  0.0 55.1 jit_solution(10951001946010231324)
XLA Ops:
  0.6 53.1 %shard_map.122.result = f32[8,128]{1,0:T(8,128)} custom-call(bf16[16,9216]{1,0:T(8,128)(2,1)} %observed.1, bf16[32,9216]{1,0:T(8,128)(2,1)} %reference_tiles.1, bf16[3,2,1536,256]{3,2,1,0:T(8,128)(2,1)} %constant.6.clone.table_in, bf16[3,3072,128]{2,1,0:T(8,128)(2,1)} %constant.7.clone.slopes_in, f32[8,4608]{1,0:T(8,128)} %constant.8.clone.freq_rows, ...), custom_call_target="tpu_custom_call" | custom-call | tf_op jit(solution)/shard_map/pallas_call | solution.py:597
  53.7 1.3 %shard_map.123 = (f32[16]{0:T(128)}, f32[3,1,40]{2,1,0:T(1,128)}) custom-call(f32[8,128]{1,0:T(8,128)} %shard_map.122.result), custom_call_target="tpu_custom_call" | custom-call | tf_op jit(solution)/shard_map/pallas_call | solution.py:658
where the time goes:
time: 55.2 us; the launch traced here: 55.1 us
  Pallas kernels  54.4 us (99%)
  between operations  0.64 us (1%)
    pallas_call x1, Pallas kernels, body(): pl.pallas_call(kernel, out_shape=jax.ShapeDtypeStruct((8, LANES), F32), i...  53.1 us
    pallas_call x1, Pallas kernels, body(): pl.pallas_call(finish, out_shape=(jax.ShapeDtypeStruct((ITEMS,), F32), ja...  1.32 us

commit v1 on v0

--- a/solution.py
+++ b/solution.py
@@ -295,6 +295,18 @@
 
     for k in (2, 1, 3):
         send_ext(k).start()
+
+    @pl.loop(0, GROUPS)
+    def _(g):
+        tile_copy(g, 0).wait()
+        tile_copy(g, 1).wait()
+
+        for half in range(2):
+
+            @pl.when((2 * g + half) % NX == x)
+            def _(half=half):
+                send_mirror((2 * g + half) // NX).start()
+
     raw_copy.wait()
 
     @pl.loop(0, GROUPS)
@@ -311,15 +323,6 @@
             items[g, y, 1, :, cols] = (im * cosine - re * sine).astype(BF16)
         for k in (2, 1, 3):
             send_item(k, g).start()
-        tile_copy(g, 0).wait()
-        tile_copy(g, 1).wait()
-
-        for half in range(2):
-
-            @pl.when((2 * g + half) % NX == x)
-            def _(half=half):
-                send_mirror((2 * g + half) // NX).start()
-
         send_near(g).start()
 
     for k in range(BLOCKS):

time: 55.2 us -> 55.2 us (level)
  no operation moved by 1% of the time
where the time goes in v1:
time: 55.2 us; the launch traced here: 55.1 us
  Pallas kernels  54.4 us (99%)
  between operations  0.64 us (1%)
    pallas_call x1, Pallas kernels, body(): pl.pallas_call(kernel, out_shape=jax.ShapeDtypeStruct((8, LANES), F32), i...  53.1 us
    pallas_call x1, Pallas kernels, body(): pl.pallas_call(finish, out_shape=(jax.ShapeDtypeStruct((ITEMS,), F32), ja...  1.32 us

profile of v1, /device:TPU:1, one launch (start us, length us, event | category | flops | bytes accessed | tf_op | source)
XLA Modules:
  0.0 55.1 jit_solution(4890435235981413668)
XLA Ops:
  0.6 53.1 %shard_map.122.result = f32[8,128]{1,0:T(8,128)} custom-call(bf16[16,9216]{1,0:T(8,128)(2,1)} %observed.1, bf16[32,9216]{1,0:T(8,128)(2,1)} %reference_tiles.1, bf16[3,2,1536,256]{3,2,1,0:T(8,128)(2,1)} %constant.6.clone.table_in, bf16[3,3072,128]{2,1,0:T(8,128)(2,1)} %constant.7.clone.slopes_in, f32[8,4608]{1,0:T(8,128)} %constant.8.clone.freq_rows, ...), custom_call_target="tpu_custom_call" | custom-call | tf_op jit(solution)/shard_map/pallas_call | solution.py:600
  53.7 1.3 %shard_map.123 = (f32[16]{0:T(128)}, f32[3,1,40]{2,1,0:T(1,128)}) custom-call(f32[8,128]{1,0:T(8,128)} %shard_map.122.result), custom_call_target="tpu_custom_call" | custom-call | tf_op jit(solution)/shard_map/pallas_call | solution.py:661
